TPU v7x, 256 devices: a whole 4x4x8 slice. The times are simulated.
256 devices in a mesh: space: 8 (over z_hi, y), dp: 32 (over x, z_lo, core).
Axes of the slice: x: 4, y: 4, z: 8 (z_hi: 2, z_lo: 4; z = z_hi * 4 + z_lo), core: 2. Of those that a mesh axis runs over, the one named last changes fastest.
Arguments:
- features: bfloat16 [32, 48, 64, 8, 128], P('dp', None, 'space'), may hold values from -21 to 21
- upstream: bfloat16 [32, 48, 64, 8, 128], P('dp', None, 'space'), may hold values from -21 to 21
- weight_one: bfloat16 [48, 48, 3, 3, 3], replicated, may hold values from -0.15625 to 0.15625
- weight_two: bfloat16 [48, 48, 3, 3, 3], replicated, may hold values from -0.15625 to 0.15625
- norm_gain: float32 [48], replicated, may hold values from 0.25 to 1.75
- norm_bias: float32 [48], replicated, may hold values from -3 to 3
Outputs:
- grad_input: bfloat16 [32, 48, 64, 8, 128], P('dp', None, 'space')
- grad_one: float32 [48, 48, 3, 3, 3], replicated
- grad_two: float32 [48, 48, 3, 3, 3], replicated
- grad_gain: float32 [48], replicated
- grad_bias: float32 [48], replicated
All inputs are finite; a program needn't handle non-finite values.
Results may differ from a plain program's by a relative error of at most 0.0029.
Values may be sent and summed in bfloat16 or wider, within the bound.
A program may use at most 128 MiB of HBM per device.

v0:
```python
import jax
import jax.numpy as jnp
from jax import lax
from jax.sharding import PartitionSpec as P

epsilon = 1e-05


def padded_2(cells, sides, width):
    for axis, dim in sides:
        count = lax.axis_size(axis)
        ends = count - 1
        head = lax.slice_in_dim(cells, 0, width, axis=dim)
        tail = lax.slice_in_dim(cells, cells.shape[dim] - width, cells.shape[dim], axis=dim)
        cells = jnp.concatenate(
            [
                lax.ppermute(tail, axis, [(i, (i + 1) % count) for i in range(ends)]),
                cells,
                lax.ppermute(head, axis, [((i + 1) % count, i) for i in range(ends)]),
            ],
            axis=dim,
        )
    return cells


def slab_faces(field):
    return padded_2(field, (("space", 2),), 1)


def conv_slab(padded, kernel):
    return lax.conv_general_dilated(
        padded,
        kernel,
        (1, 1, 1),
        ((0, 0), (1, 1), (1, 1)),
        dimension_numbers=("NCDHW", "OIDHW", "NCDHW"),
        preferred_element_type=jnp.float32,
    )


def flipped(kernel):
    return jnp.transpose(kernel, (1, 0, 2, 3, 4))[:, :, ::-1, ::-1, ::-1]


def kernel_grad(padded, target):
    return lax.conv_general_dilated(
        padded,
        target,
        (1, 1, 1),
        ((0, 0), (1, 1), (1, 1)),
        dimension_numbers=("CNDHW", "IODHW", "CNDHW"),
        preferred_element_type=jnp.float32,
    )


def local(features, upstream, weight_one, weight_two, norm_gain, norm_bias):
    axes_cells = (2, 3, 4)
    cells_all = float(
        features.shape[2] * features.shape[3] * features.shape[4] * lax.axis_size("space")
    )
    padded_x = slab_faces(features)
    pre_act = conv_slab(padded_x, weight_one)
    sums_pre, squares_pre = lax.psum(
        (
            jnp.sum(pre_act, axis=axes_cells, keepdims=True),
            jnp.sum(pre_act * pre_act, axis=axes_cells, keepdims=True),
        ),
        "space",
    )
    mean_pre = sums_pre / cells_all
    inv_std = lax.rsqrt(squares_pre / cells_all - mean_pre * mean_pre + epsilon)
    normal_hat = (pre_act - mean_pre) * inv_std
    gain_b = norm_gain.reshape(1, -1, 1, 1, 1)
    normed = normal_hat * gain_b + norm_bias.reshape(1, -1, 1, 1, 1)
    sigmoid_val = jax.nn.sigmoid(normed)
    hidden = (normed * sigmoid_val).astype(jnp.bfloat16)
    padded_h = slab_faces(hidden)
    padded_g = slab_faces(upstream)
    local_two = kernel_grad(padded_h, upstream)
    grad_hidden = conv_slab(padded_g, flipped(weight_two))
    grad_norm = grad_hidden * sigmoid_val * (1.0 + normed * (1.0 - sigmoid_val))
    local_bias = jnp.sum(grad_norm, axis=(0, 2, 3, 4))
    local_gain = jnp.sum(grad_norm * normal_hat, axis=(0, 2, 3, 4))
    slope_sum, slope_dot = lax.psum(
        (
            jnp.sum(grad_norm, axis=axes_cells, keepdims=True),
            jnp.sum(grad_norm * normal_hat, axis=axes_cells, keepdims=True),
        ),
        "space",
    )
    grad_pre = (
        gain_b
        * inv_std
        * (grad_norm - slope_sum / cells_all - normal_hat * (slope_dot / cells_all))
    ).astype(jnp.bfloat16)
    padded_grad = slab_faces(grad_pre)
    local_one = kernel_grad(padded_x, grad_pre)
    back = conv_slab(padded_grad, flipped(weight_one))
    grad_input = (upstream.astype(jnp.float32) + back).astype(jnp.bfloat16)
    grad_one, grad_two, grad_gain, grad_bias = lax.psum(
        (local_one, local_two, local_gain, local_bias), ("space", "dp")
    )
    return (grad_input, grad_one, grad_two, grad_gain, grad_bias)


def solution(mesh):
    in_specs = (
        P("dp", None, "space", None, None),
        P("dp", None, "space", None, None),
        P(),
        P(),
        P(),
        P(),
    )
    out_specs = (P("dp", None, "space", None, None), P(), P(), P(), P())
    return jax.shard_map(local, mesh=mesh, in_specs=in_specs, out_specs=out_specs, check_vma=False)
```

profile of v0, /device:TPU:1, one launch (start us, length us, event | category | flops | bytes accessed | tf_op | source)
XLA Modules:
  0.0 684.3 jit_solution(1534281291638809892)
XLA Ops:
  7.2 0.0 copy-start
  7.2 0.0 copy-start.5
  7.2 0.0 all-reduce.6.cloned.1.call-start
  7.2 1.0 fusion.73
  8.3 4.2 collective-permute-start
  12.5 1.3 collective-permute-start.1
  13.8 1.6 fusion.74
  15.4 4.6 collective-permute-start.2
  20.0 1.3 collective-permute-start.3
  21.3 7.4 %copy.112 = bf16[1,48,8,8,128]{1,0,4,3,2:T(2,128)(2,1)} copy(bf16[1,48,8,8,128]{4,3,2,1,0:T(8,128)(2,1)} %param.7) | data formatting | bytes 1572864 | tf_op args[1]
  28.7 2.5 copy.85
  31.2 0.1 pad_maximum_fusion.2
  31.3 3.5 copy.86
  34.8 3.6 fusion.70
  38.4 3.1 fusion.68
  41.5 0.1 fusion.69
  41.6 0.5 copy.88
  42.1 1.5 copy-done.10
  43.6 0.8 slice.50
  44.4 2.0 pad_maximum_fusion.3
  46.5 4.9 copy.89
  51.3 2.3 pad.2
  53.7 0.0 copy-start.14
  53.7 0.5 copy.91
  54.2 0.8 slice.51
  55.0 1.2 copy-done.11
  56.3 0.3 copy-done.13
  56.6 12.1 %select_reduce_fusion.3 = (f32[48]{0:T(128)S(1)}, f32[48]{0:T(128)S(1)}, f32[8,8,8,17,48]{4,2,3,1,0:T(8,128)}) fusion(pred[8,17]{0,1:T(8,128)(4,1)S(1)} %copy-done.14, bf16[48,48,3,3,3]{1,0,4,3,2:T(8,128)(2,1)S(1)} %copy-done, bf16[48,10,8,1,7,2]{0,4,5,2,1,3:T(8,128)(2,1)S(1)} %copy-done.13, bf16[48,10,8,1,8,17]{0,4,5,2,1,3:T(8,128)(2,1)S(1)} %copy-done.11), kind=kOutput, calls=%fused_computation.25 | convolution fusion | flops 998682496 | bytes 2948104 | tf_op jit(solution)/shard_map/conv_general_dilated | solution.py:31
  68.7 30.8 %all-reduce.3 = (f32[1,48,1,1,1]{1,4,3,2,0:T(1,128)S(1)}, f32[1,48,1,1,1]{1,4,3,2,0:T(1,128)S(1)}) all-reduce(f32[1,48,1,1,1]{1,4,3,2,0:T(1,128)S(1)} %bitcast.113, f32[1,48,1,1,1]{1,4,3,2,0:T(1,128)S(1)} %bitcast.112), channel_id=1, replica_groups=mesh['space'=8,'dp'=32] {'space'}, use_global_device_ids=true, to_apply=%region_1.0 | all-reduce | flops 96 | bytes 768 | tf_op jit(solution)/shard_map/psum | solution.py:63
  99.5 16.4 %select_reduce_fusion = (f32[48]{0:T(128)S(1)}, f32[48]{0:T(128)S(1)}, f32[8,8,8,17,48]{4,2,3,1,0:T(8,128)}) fusion(pred[8,17]{0,1:T(8,128)(4,1)S(1)} %copy-done.14, f32[48]{0:T(128)S(1)} %bitcast.108, f32[48]{0:T(128)S(1)} %get-tuple-element.55, f32[8,8,8,17,48]{4,2,3,1,0:T(8,128)} %get-tuple-element.56, f32[48]{0:T(128)S(1)} %copy-done.16, ...), kind=kOutput, calls=%fused_computation.17 | convolution fusion | flops 1004113792 | bytes 4620040 | tf_op jit(solution)/shard_map/conv_general_dilated | solution.py:31
  115.9 25.0 %all-reduce.2 = (f32[1,48,1,1,1]{1,4,3,2,0:T(1,128)S(1)}, f32[1,48,1,1,1]{1,4,3,2,0:T(1,128)S(1)}) all-reduce(f32[1,48,1,1,1]{1,4,3,2,0:T(1,128)S(1)} %bitcast.111, f32[1,48,1,1,1]{1,4,3,2,0:T(1,128)S(1)} %bitcast.110), channel_id=1, replica_groups=mesh['space'=8,'dp'=32] {'space'}, use_global_device_ids=true, to_apply=%region_5.0 | all-reduce | flops 96 | bytes 768 | tf_op jit(solution)/shard_map/psum | solution.py:84
  140.9 4.9 multiply_convert_fusion.1
  145.8 0.3 copy.93
  146.3 1.2 copy.128
  147.5 2.2 collective-permute-start.6
  149.8 1.2 copy.127
  151.0 1.3 collective-permute-start.7
  152.3 2.3 copy.117
  154.6 2.3 copy.118
  156.9 1.9 copy.104
  159.0 4.0 collective-permute-start.4
  163.0 1.3 collective-permute-start.5
  164.3 1.5 fusion.36
  165.9 17.9 %fusion.49 = f32[48,48,3,3,3]{0,1,4,3,2:T(8,128)} fusion(bf16[8,8,8,17,48]{4,2,3,1,0:T(8,128)(2,1)S(1)} %get-tuple-element.40, pred[8,17]{0,1:T(8,128)(4,1)S(1)} %copy-done.14, bf16[48,10,8,8,17,1]{0,3,5,4,2,1:T(8,128)(2,1)S(1)} %get-tuple-element.60, bf16[48,10,8,8,17,1]{0,3,5,4,2,1:T(8,128)(2,1)} %copy.104, ...), kind=kOutput, calls=%fused_computation.61 | convolution fusion | flops 1002491904 | bytes 4217992 | tf_op jit(solution)/shard_map/conv_general_dilated | solution.py:46
  183.8 0.1 slice_bitcast_fusion.1
  183.9 0.3 copy.108
  184.2 0.1 slice.65
  184.3 6.4 copy.126
  190.7 101.2 %all-reduce = (f32[48]{0:T(128)}, f32[48]{0:T(128)}) all-reduce(f32[48]{0:T(128)S(1)} %get-tuple-element.25, f32[48]{0:T(128)S(1)} %get-tuple-element.26), channel_id=1, replica_groups=mesh['space'=8,'dp'=32] {'space','dp'}, use_global_device_ids=true, to_apply=%region_10.0 | all-reduce | flops 96 | bytes 768 | tf_op jit(solution)/shard_map/psum | solution.py:100
  291.9 0.6 maximum_bitcast_fusion
  292.5 0.6 pad.7
  293.1 0.5 copy.98
  293.6 0.1 slice.57
  293.7 10.5 %broadcast_select_fusion = f32[8,8,8,17,48]{4,2,3,1,0:T(8,128)S(1)} fusion(pred[8,17]{0,1:T(8,128)(4,1)S(1)} %copy-done.14, bf16[48,48,3,3,3]{1,0,4,3,2:T(8,128)(2,1)S(1)} %copy-done, bf16[48,10,8,1,7,2]{0,4,5,2,1,3:T(8,128)(2,1)S(1)} %slice.57, bf16[48,10,8,1,8,17]{0,4,5,2,1,3:T(8,128)(2,1)S(1)} %copy.98), kind=kOutput, calls=%fused_computation.55 | convolution fusion | flops 996593664 | bytes 2947720 | tf_op jit(solution)/shard_map/conv_general_dilated | solution.py:31
  304.2 3.1 copy.99
  307.3 0.2 copy-done.7
  307.4 1.8 copy-done.8
  309.3 110.6 %fusion.11 = f32[48,48,3,3,3]{0,1,4,3,2:T(8,128)} fusion(bf16[1,48,8,8,128]{1,0,4,3,2:T(2,128)(2,1)S(1)} %copy-done.7, bf16[1,48,1,8,128]{1,0,4,3,2:T(2,128)(2,1)} %collective-permute-done.7, bf16[1,48,8,8,128]{1,0,4,3,2:T(2,128)(2,1)S(1)} %bitcast.102, bf16[1,48,1,8,128]{1,0,4,3,2:T(2,128)(2,1)} %collective-permute-done.6), kind=kOutput, calls=%fused_computation.15 | convolution fusion | flops 932364288 | bytes 2018304 | tf_op jit(solution)/shard_map/conv_general_dilated | solution.py:46
  419.8 0.0 all-reduce.6.cloned.1.call-update
  419.9 4.1 fusion.13
  424.0 3.8 copy.113
  427.8 245.1 %all-reduce.6.cloned.1.call-done = (f32[48,48,3,3,3]{0,1,4,3,2:T(8,128)}, f32[48,48,3,3,3]{0,1,4,3,2:T(8,128)}) async-done(((f32[48,48,3,3,3]{0,1,4,3,2:T(8,128)}, f32[48,48,3,3,3]{0,1,4,3,2:T(8,128)}), (f32[48,48,3,3,3]{0,1,4,3,2:T(8,128)}, f32[48,48,3,3,3]{0,1,4,3,2:T(8,128)})) %all-reduce.6.cloned.1.call-update) | async-done | bytes 497680 | tf_op jit(solution)/shard_map/psum | solution.py:100
  672.9 2.2 copy.114
  675.1 2.2 copy.115
  (48 shorter events, 0.5 us)
Async XLA Ops:
  7.2 47.9 %copy-start = (bf16[48,48,3,3,3]{1,0,4,3,2:T(8,128)(2,1)S(1)}, bf16[48,48,3,3,3]{1,0,4,3,2:T(8,128)(2,1)}, u32[]{:S(2)}) copy-start(bf16[48,48,3,3,3]{1,0,4,3,2:T(8,128)(2,1)} %param.8) | copy-start | bytes 373252
  7.2 21.5 %copy-start.5 = (bf16[1,48,8,8,128]{4,3,2,1,0:T(8,128)(2,1)S(1)}, bf16[1,48,8,8,128]{4,3,2,1,0:T(8,128)(2,1)}, u32[]{:S(2)}) copy-start(bf16[1,48,8,8,128]{4,3,2,1,0:T(8,128)(2,1)} %param.7) | copy-start | bytes 2359300
  7.2 665.7 %all-reduce.6.cloned.1.call-start = ((), (), s32[]{:S(2)}) async-start(), calls=%async_computation | async-start | bytes 2654208 | tf_op jit(solution)/shard_map/psum | solution.py:100
  8.3 22.9 %copy-start.12 = (bf16[1,48,8,8,128]{4,3,2,1,0:T(8,128)(2,1)S(1)}, bf16[1,48,8,8,128]{4,3,2,1,0:T(8,128)(2,1)}, u32[]{:S(2)}) copy-start(bf16[1,48,8,8,128]{4,3,2,1,0:T(8,128)(2,1)} %param.6) | copy-start | bytes 2359300
  8.3 22.9 %collective-permute-start = (bf16[1,48,1,8,128]{4,3,2,1,0:T(8,128)(2,1)S(1)}, bf16[1,48,1,8,128]{4,3,2,1,0:T(8,128)(2,1)S(1)}, u32[]{:S(2)}, u32[]{:S(2)}) collective-permute-start(bf16[1,48,1,8,128]{4,3,2,1,0:T(8,128)(2,1)S(1)} %get-tuple-element.51), channel_id=1, source_target_pairs={{0,32},{32,64},{64,96},{96,128},{128,160},{160,192},{192,224},{1,3... | collective-permute-start | bytes 294920 | tf_op jit(solution)/shard_map/ppermute | solution.py:17
  12.5 18.7 %collective-permute-start.1 = (bf16[1,48,1,8,128]{4,3,2,1,0:T(8,128)(2,1)S(1)}, bf16[1,48,1,8,128]{4,3,2,1,0:T(8,128)(2,1)S(1)}, u32[]{:S(2)}, u32[]{:S(2)}) collective-permute-start(bf16[1,48,1,8,128]{4,3,2,1,0:T(8,128)(2,1)S(1)} %get-tuple-element.52), channel_id=1, source_target_pairs={{32,0},{64,32},{96,64},{128,96},{160,128},{192,160},{224,192},{33,... | collective-permute-start | bytes 294920 | tf_op jit(solution)/shard_map/ppermute | solution.py:19
  15.4 29.1 %collective-permute-start.2 = (bf16[1,48,1,8,128]{4,3,2,1,0:T(8,128)(2,1)}, bf16[1,48,1,8,128]{4,3,2,1,0:T(8,128)(2,1)}, u32[]{:S(2)}, u32[]{:S(2)}) collective-permute-start(bf16[1,48,1,8,128]{4,3,2,1,0:T(8,128)(2,1)} %get-tuple-element.53), channel_id=1, source_target_pairs={{0,32},{32,64},{64,96},{96,128},{128,160},{160,192},{192,224},{1,3... | collective-permute-start | bytes 294920 | tf_op jit(solution)/shard_map/ppermute | solution.py:17
  20.0 24.4 %collective-permute-start.3 = (bf16[1,48,1,8,128]{4,3,2,1,0:T(8,128)(2,1)S(1)}, bf16[1,48,1,8,128]{4,3,2,1,0:T(8,128)(2,1)}, u32[]{:S(2)}, u32[]{:S(2)}) collective-permute-start(bf16[1,48,1,8,128]{4,3,2,1,0:T(8,128)(2,1)S(1)} %get-tuple-element.54), channel_id=1, source_target_pairs={{32,0},{64,32},{96,64},{128,96},{160,128},{192,160},{224,192},{33,... | collective-permute-start | bytes 294920 | tf_op jit(solution)/shard_map/ppermute | solution.py:19
  41.5 2.9 copy-start.6
  42.1 1.6 copy-start.10
  53.7 2.6 copy-start.11
  53.7 2.8 copy-start.13
  53.7 2.8 copy-start.14
  54.2 14.5 %copy-start.9 = (bf16[48,10,8,1,8,17]{0,4,5,2,1,3:T(8,128)(2,1)}, bf16[48,10,8,1,8,17]{0,4,5,2,1,3:T(8,128)(2,1)S(1)}, u32[]{:S(2)}) copy-start(bf16[48,10,8,1,8,17]{0,4,5,2,1,3:T(8,128)(2,1)S(1)} %copy.91) | copy-start | bytes 3133444
  56.5 43.0 %copy-start.15 = (f32[48]{0:T(128)S(1)}, f32[48]{0:T(128)}, u32[]{:S(2)}) copy-start(f32[48]{0:T(128)} %param.10) | copy-start | bytes 580
  56.5 43.0 %copy-start.16 = (f32[48]{0:T(128)S(1)}, f32[48]{0:T(128)}, u32[]{:S(2)}) copy-start(f32[48]{0:T(128)} %param.11) | copy-start | bytes 580
  145.8 6.5 copy-start.3
  146.2 8.3 %copy-start.2 = (bf16[48,10,8,1,8,16]{0,2,5,4,1,3:T(8,128)(2,1)S(1)}, bf16[48,10,8,1,8,16]{0,2,5,4,1,3:T(8,128)(2,1)}, u32[]{:S(2)}) copy-start(bf16[48,10,8,1,8,16]{0,2,5,4,1,3:T(8,128)(2,1)} %get-tuple-element.42) | copy-start | bytes 2949124
  147.5 159.8 %collective-permute-start.6 = (bf16[1,48,1,8,128]{1,0,4,3,2:T(2,128)(2,1)}, bf16[1,48,1,8,128]{1,0,4,3,2:T(2,128)(2,1)}, u32[]{:S(2)}, u32[]{:S(2)}) collective-permute-start(bf16[1,48,1,8,128]{1,0,4,3,2:T(2,128)(2,1)} %bitcast.90), channel_id=1, source_target_pairs={{0,32},{32,64},{64,96},{96,128},{128,160},{160,192},{192,224},{1,3... | collective-permute-start | bytes 294920 | tf_op jit(solution)/shard_map/ppermute | solution.py:17
  151.0 156.3 %collective-permute-start.7 = (bf16[1,48,1,8,128]{1,0,4,3,2:T(2,128)(2,1)}, bf16[1,48,1,8,128]{1,0,4,3,2:T(2,128)(2,1)}, u32[]{:S(2)}, u32[]{:S(2)}) collective-permute-start(bf16[1,48,1,8,128]{1,0,4,3,2:T(2,128)(2,1)} %bitcast.89), channel_id=1, source_target_pairs={{32,0},{64,32},{96,64},{128,96},{160,128},{192,160},{224,192},{33,... | collective-permute-start | bytes 294920 | tf_op jit(solution)/shard_map/ppermute | solution.py:19
  159.0 132.9 %collective-permute-start.4 = (bf16[1,48,1,8,128]{1,3,4,0,2:T(8,128)(2,1)S(1)}, bf16[1,48,1,8,128]{1,3,4,0,2:T(8,128)(2,1)S(1)}, u32[]{:S(2)}, u32[]{:S(2)}) collective-permute-start(bf16[1,48,1,8,128]{1,3,4,0,2:T(8,128)(2,1)S(1)} %slice_bitcast_fusion.3), channel_id=1, source_target_pairs={{0,32},{32,64},{64,96},{96,128},{128,160},{160,192},{192,224},{1,3... | collective-permute-start | bytes 294920 | tf_op jit(solution)/shard_map/ppermute | solution.py:17
  163.0 128.9 %collective-permute-start.5 = (bf16[1,48,1,8,128]{1,3,4,2,0:T(8,128)(2,1)S(1)}, bf16[1,48,1,8,128]{1,3,4,2,0:T(8,128)(2,1)S(1)}, u32[]{:S(2)}, u32[]{:S(2)}) collective-permute-start(bf16[1,48,1,8,128]{1,3,4,2,0:T(8,128)(2,1)S(1)} %slice_bitcast_fusion.2), channel_id=1, source_target_pairs={{32,0},{64,32},{96,64},{128,96},{160,128},{192,160},{224,192},{33,... | collective-permute-start | bytes 294920 | tf_op jit(solution)/shard_map/ppermute | solution.py:19
  304.2 3.3 copy-start.7
  304.2 5.1 copy-start.8
  309.2 110.6 %copy-start.4 = (bf16[1,48,8,8,128]{1,3,4,2,0:T(8,128)(2,1)S(1)}, bf16[1,48,8,8,128]{1,3,4,2,0:T(8,128)(2,1)}, u32[]{:S(2)}) copy-start(bf16[1,48,8,8,128]{1,3,4,2,0:T(8,128)(2,1)} %copy.85) | copy-start | bytes 2359300
  419.9 257.4 %copy-start.1 = (bf16[48,48,3,3,3]{1,0,4,3,2:T(8,128)(2,1)S(1)}, bf16[48,48,3,3,3]{1,0,4,3,2:T(8,128)(2,1)}, u32[]{:S(2)}) copy-start(bf16[48,48,3,3,3]{1,0,4,3,2:T(8,128)(2,1)} %param.8) | copy-start | bytes 373252
Sparse Core Ops, SparseCore 0:
  420.0 252.9 all-reduce.5
where the time goes:
time: 690 us; the launch traced here: 684 us
  waiting for transfers between devices  245 us (36%)
  matrix products  167 us (24%)
  blocking collectives  157 us (23%)
  local copies, waits for them, and re-layouts  66.6 us (10%)
  starting transfers between devices  20.2 us (3%)
  between operations  14.7 us (2%)
  other arithmetic  13.3 us (2%)
    psum x1, waiting for transfers between devices, local(): lax.psum((local_one, local_two, local_gain, local_bias), ('space', 'dp'))  245 us
    conv_general_dilated x2, matrix products, kernel_grad(): lax.conv_general_dilated(padded, target, (1, 1, 1), ((0, 0), (1, 1), (1,...  128 us
    psum x1, blocking collectives, local(): lax.psum((local_one, local_two, local_gain, local_bias), ('space', 'dp'))  101 us
    conv_general_dilated x3, matrix products, conv_slab(): lax.conv_general_dilated(padded, kernel, (1, 1, 1), ((0, 0), (1, 1), (1,...  39 us
    unnamed x46, local copies, waits for them, and re-layouts  36.6 us
    psum x1, blocking collectives, local(): lax.psum((jnp.sum(pre_act, axis=axes_cells, keepdims=True), jnp.sum(pre_a...  30.8 us
    psum x1, blocking collectives, local(): lax.psum((jnp.sum(grad_norm, axis=axes_cells, keepdims=True), jnp.sum(gra...  25 us
    concatenate x8, local copies, waits for them, and re-layouts, padded_2(): jnp.concatenate([lax.ppermute(tail, axis, [(i, (i + 1) % count) for i in...  20 us
  transfers between devices with their start and end apart: 9, of which 1 were waited for; matrix products, arithmetic and copies ran while one was open for 12% of the time, Pallas kernels for 0%

commit v1 on v0

--- a/solution.py
+++ b/solution.py
@@ -98,7 +98,7 @@
     back = conv_slab(padded_grad, flipped(weight_one))
     grad_input = (upstream.astype(jnp.float32) + back).astype(jnp.bfloat16)
     grad_one, grad_two, grad_gain, grad_bias = lax.psum(
-        (local_one, local_two, local_gain, local_bias), ("space", "dp")
+        lax.psum((local_one, local_two, local_gain, local_bias), "space"), "dp"
     )
     return (grad_input, grad_one, grad_two, grad_gain, grad_bias)
 

time: 690 us -> 701 us (1.016)
  waiting for transfers between devices: 245 us -> 316 us
  matrix products: 167 us -> 130 us
  blocking collectives: 157 us -> 136 us
    psum x1 -> x2, waiting for transfers between devices: 245 us -> 316 us  [the longest x1 265 us: local(): lax.psum(lax.psum((local_one, local_two, local_gain, local_bias), 'space'...]
    conv_general_dilated x2, matrix products: 128 us -> 91.3 us  [kernel_grad(): lax.conv_general_dilated(padded, target, (1, 1, 1), ((0, 0), (1, 1), (1,...]
    psum x1, blocking collectives: 101 us -> 79.9 us  [local(): lax.psum(lax.psum((local_one, local_two, local_gain, local_bias), 'space'...]
    unnamed x46 -> x52, local copies, waits for them, and re-layouts: 36.6 us -> 34.2 us
  transfers between devices with their start and end apart: 9 -> 10, of which waited for: 1 -> 2; matrix products, arithmetic and copies ran while one was open for 12% -> 22% of each run, Pallas kernels for 0% -> 0%
where the time goes in v1:
time: 701 us; the launch traced here: 696 us
  waiting for transfers between devices  316 us (45%)
  blocking collectives  136 us (19%)
  matrix products  130 us (19%)
  local copies, waits for them, and re-layouts  66.4 us (9%)
  starting transfers between devices  21 us (3%)
  between operations  14.9 us (2%)
  other arithmetic  11.3 us (2%)
    psum x1, waiting for transfers between devices, local(): lax.psum(lax.psum((local_one, local_two, local_gain, local_bias), 'space'...  265 us
    conv_general_dilated x2, matrix products, kernel_grad(): lax.conv_general_dilated(padded, target, (1, 1, 1), ((0, 0), (1, 1), (1,...  91.3 us
    psum x1, blocking collectives, local(): lax.psum(lax.psum((local_one, local_two, local_gain, local_bias), 'space'...  79.9 us
    psum x1, waiting for transfers between devices, local(): lax.psum((local_one, local_two, local_gain, local_bias), 'space')  51.7 us
    conv_general_dilated x3, matrix products, conv_slab(): lax.conv_general_dilated(padded, kernel, (1, 1, 1), ((0, 0), (1, 1), (1,...  38.6 us
    unnamed x52, local copies, waits for them, and re-layouts  34.2 us
    psum x1, blocking collectives, local(): lax.psum((jnp.sum(pre_act, axis=axes_cells, keepdims=True), jnp.sum(pre_a...  30.6 us
    psum x1, blocking collectives, local(): lax.psum((jnp.sum(grad_norm, axis=axes_cells, keepdims=True), jnp.sum(gra...  25.5 us
  transfers between devices with their start and end apart: 10, of which 2 were waited for; matrix products, arithmetic and copies ran while one was open for 22% of the time, Pallas kernels for 0%

profile of v1, /device:TPU:1, one launch (start us, length us, event | category | flops | bytes accessed | tf_op | source)
XLA Modules:
  0.0 695.7 jit_solution(1503938439072407728)
XLA Ops:
  7.2 0.0 all-reduce.10.cloned.1.call-start
  7.2 1.0 fusion.73
  8.3 4.2 collective-permute-start
  12.5 1.3 collective-permute-start.1
  13.8 1.6 fusion.74
  15.4 4.6 collective-permute-start.2
  20.0 1.3 collective-permute-start.3
  21.3 7.4 %copy.112 = bf16[1,48,8,8,128]{1,0,4,3,2:T(2,128)(2,1)} copy(bf16[1,48,8,8,128]{4,3,2,1,0:T(8,128)(2,1)} %param.7) | data formatting | bytes 1572864 | tf_op args[1]
  28.7 2.6 copy.85
  31.2 0.1 pad_maximum_fusion.2
  31.3 3.5 copy.86
  34.8 3.6 fusion.70
  38.4 3.2 fusion.68
  41.6 0.1 fusion.69
  41.6 0.5 copy.88
  42.1 1.5 copy-done.9
  43.6 0.8 slice.50
  44.5 2.0 pad_maximum_fusion.3
  46.5 5.1 copy.89
  51.6 2.3 pad.2
  54.0 0.5 copy.91
  54.5 0.8 slice.51
  55.3 1.2 copy-done.10
  56.6 0.3 copy-done.13
  56.9 12.2 %select_reduce_fusion.3 = (f32[48]{0:T(128)S(1)}, f32[48]{0:T(128)S(1)}, f32[8,8,8,17,48]{4,2,3,1,0:T(8,128)}) fusion(pred[8,17]{0,1:T(8,128)(4,1)S(1)} %copy-done.14, bf16[48,48,3,3,3]{1,0,4,3,2:T(8,128)(2,1)S(1)} %copy-done, bf16[48,10,8,1,7,2]{0,4,5,2,1,3:T(8,128)(2,1)S(1)} %copy-done.13, bf16[48,10,8,1,8,17]{0,4,5,2,1,3:T(8,128)(2,1)S(1)} %copy-done.10), kind=kOutput, calls=%fused_computation.25 | convolution fusion | flops 998682496 | bytes 2948104 | tf_op jit(solution)/shard_map/conv_general_dilated | solution.py:31
  69.0 30.6 %all-reduce.3 = (f32[1,48,1,1,1]{1,4,3,2,0:T(1,128)S(1)}, f32[1,48,1,1,1]{1,4,3,2,0:T(1,128)S(1)}) all-reduce(f32[1,48,1,1,1]{1,4,3,2,0:T(1,128)S(1)} %bitcast.112, f32[1,48,1,1,1]{1,4,3,2,0:T(1,128)S(1)} %bitcast.111), channel_id=1, replica_groups=mesh['space'=8,'dp'=32] {'space'}, use_global_device_ids=true, to_apply=%region_1.0 | all-reduce | flops 96 | bytes 768 | tf_op jit(solution)/shard_map/psum | solution.py:63
  99.6 16.4 %select_reduce_fusion = (f32[48]{0:T(128)S(1)}, f32[48]{0:T(128)S(1)}, f32[8,8,8,17,48]{4,2,3,1,0:T(8,128)}) fusion(pred[8,17]{0,1:T(8,128)(4,1)S(1)} %copy-done.14, f32[48]{0:T(128)S(1)} %bitcast.107, f32[48]{0:T(128)S(1)} %get-tuple-element.59, f32[8,8,8,17,48]{4,2,3,1,0:T(8,128)} %get-tuple-element.60, f32[48]{0:T(128)S(1)} %copy-done.17, ...), kind=kOutput, calls=%fused_computation.17 | convolution fusion | flops 1004113792 | bytes 4620040 | tf_op jit(solution)/shard_map/conv_general_dilated | solution.py:31
  116.0 25.5 %all-reduce.2 = (f32[1,48,1,1,1]{1,4,3,2,0:T(1,128)S(1)}, f32[1,48,1,1,1]{1,4,3,2,0:T(1,128)S(1)}, f32[48]{0:T(128)}, f32[48]{0:T(128)}) all-reduce(f32[1,48,1,1,1]{1,4,3,2,0:T(1,128)S(1)} %bitcast.110, f32[1,48,1,1,1]{1,4,3,2,0:T(1,128)S(1)} %bitcast.109, f32[48]{0:T(128)S(1)} %get-tuple-element.25, ...), channel_id=1, replica_groups=mesh['space'=8,'dp'=32] {'space'}, use_global_device_ids=true, to_apply=%region_5.0 | all-reduce | flops 192 | bytes 1536 | tf_op jit(solution)/shard_map/psum | solution.py:84
  141.5 4.9 multiply_convert_fusion.1
  146.4 1.7 copy.93
  148.3 1.2 copy.128
  149.5 2.1 collective-permute-start.6
  151.6 1.2 copy.127
  152.8 1.3 collective-permute-start.7
  154.1 2.3 copy.117
  156.4 2.3 copy.118
  158.8 1.9 copy.104
  160.8 0.7 slice_bitcast_fusion.3
  161.5 4.7 collective-permute-start.4
  166.2 0.7 slice_bitcast_fusion.2
  167.0 1.5 collective-permute-start.5
  168.5 1.6 fusion.36
  170.1 16.3 %fusion.49 = f32[48,48,3,3,3]{0,1,4,3,2:T(8,128)} fusion(bf16[8,8,8,17,48]{4,2,3,1,0:T(8,128)(2,1)S(1)} %get-tuple-element.44, pred[8,17]{0,1:T(8,128)(4,1)S(1)} %copy-done.14, bf16[48,10,8,8,17,1]{0,3,5,4,2,1:T(8,128)(2,1)S(1)} %get-tuple-element.64, bf16[48,10,8,8,17,1]{0,3,5,4,2,1:T(8,128)(2,1)S(1)} %copy-done.11, ...), kind=kOutput, calls=%fused_computation.61 | convolution fusion | flops 1002491904 | bytes 4217992 | tf_op jit(solution)/shard_map/conv_general_dilated | solution.py:46
  186.4 0.3 copy.108
  186.7 0.1 slice.65
  186.8 6.3 copy.126
  193.2 75.0 %fusion.11 = f32[48,48,3,3,3]{0,1,4,3,2:T(8,128)} fusion(bf16[1,48,8,8,128]{1,0,4,3,2:T(2,128)(2,1)S(1)} %copy-done.7, bf16[1,48,1,8,128]{1,0,4,3,2:T(2,128)(2,1)} %collective-permute-done.7, bf16[1,48,8,8,128]{1,0,4,3,2:T(2,128)(2,1)} %bitcast.102, bf16[1,48,1,8,128]{1,0,4,3,2:T(2,128)(2,1)} %collective-permute-done.6), kind=kOutput, calls=%fused_computation.15 | convolution fusion | flops 932364288 | bytes 2018304 | tf_op jit(solution)/shard_map/conv_general_dilated | solution.py:46
  268.2 0.0 all-reduce.10.cloned.1.call-update
  268.2 0.0 all-reduce.8.cloned.1.call-start
  268.3 1.5 slice_bitcast_fusion.1
  269.8 79.9 %all-reduce = (f32[48]{0:T(128)}, f32[48]{0:T(128)}) all-reduce(f32[48]{0:T(128)S(1)} %copy-done.18, f32[48]{0:T(128)S(1)} %copy-done.19), channel_id=1, replica_groups=mesh['space'=8,'dp'=32] {'dp'}, use_global_device_ids=true, to_apply=%region_13.0 | all-reduce | flops 96 | bytes 768 | tf_op jit(solution)/shard_map/psum | solution.py:100
  349.7 2.3 maximum_bitcast_fusion
  352.0 0.6 pad.7
  352.5 0.5 copy.98
  353.0 0.1 slice.57
  353.1 51.7 %all-reduce.10.cloned.1.call-done = (f32[48,48,3,3,3]{0,1,4,3,2:T(8,128)}, f32[48,48,3,3,3]{0,1,4,3,2:T(8,128)}) async-done(((f32[48,48,3,3,3]{0,1,4,3,2:T(8,128)}, f32[48,48,3,3,3]{0,1,4,3,2:T(8,128)}), (f32[48,48,3,3,3]{0,1,4,3,2:T(8,128)}, f32[48,48,3,3,3]{0,1,4,3,2:T(8,128)})) %all-reduce.10.cloned.1.call-update) | async-done | bytes 497680 | tf_op jit(solution)/shard_map/psum | solution.py:101
  404.8 10.1 %broadcast_select_fusion = f32[8,8,8,17,48]{4,2,3,1,0:T(8,128)S(1)} fusion(pred[8,17]{0,1:T(8,128)(4,1)S(1)} %copy-done.15, bf16[48,48,3,3,3]{1,0,4,3,2:T(8,128)(2,1)S(1)} %copy-done, bf16[48,10,8,1,7,2]{0,4,5,2,1,3:T(8,128)(2,1)S(1)} %slice.57, bf16[48,10,8,1,8,17]{0,4,5,2,1,3:T(8,128)(2,1)S(1)} %copy.98), kind=kOutput, calls=%fused_computation.55 | convolution fusion | flops 996593664 | bytes 2947720 | tf_op jit(solution)/shard_map/conv_general_dilated | solution.py:31
  414.9 0.8 copy.99
  415.7 0.8 copy-done.4
  416.5 0.4 fusion.13
  416.9 2.7 copy.113
  419.6 264.5 %all-reduce.8.cloned.1.call-done = (f32[48,48,3,3,3]{0,1,4,3,2:T(8,128)}, f32[48,48,3,3,3]{0,1,4,3,2:T(8,128)}) async-done(((f32[48,48,3,3,3]{0,1,4,3,2:T(8,128)}, f32[48,48,3,3,3]{0,1,4,3,2:T(8,128)}), (f32[48,48,3,3,3]{0,1,4,3,2:T(8,128)}, f32[48,48,3,3,3]{0,1,4,3,2:T(8,128)})) %all-reduce.8.cloned.1.call-update) | async-done | bytes 497680 | tf_op jit(solution)/shard_map/psum | solution.py:100
  684.1 2.2 copy.114
  686.3 2.2 copy.115
  (57 shorter events, 0.5 us)
Async XLA Ops:
  7.2 48.2 %copy-start = (bf16[48,48,3,3,3]{1,0,4,3,2:T(8,128)(2,1)S(1)}, bf16[48,48,3,3,3]{1,0,4,3,2:T(8,128)(2,1)}, u32[]{:S(2)}) copy-start(bf16[48,48,3,3,3]{1,0,4,3,2:T(8,128)(2,1)} %param.8) | copy-start | bytes 373252
  7.2 21.5 %copy-start.5 = (bf16[1,48,8,8,128]{4,3,2,1,0:T(8,128)(2,1)S(1)}, bf16[1,48,8,8,128]{4,3,2,1,0:T(8,128)(2,1)}, u32[]{:S(2)}) copy-start(bf16[1,48,8,8,128]{4,3,2,1,0:T(8,128)(2,1)} %param.7) | copy-start | bytes 2359300
  7.2 397.6 %all-reduce.10.cloned.1.call-start = ((), (), s32[]{:S(2)}) async-start(), calls=%async_computation.1 | async-start | bytes 2654208 | tf_op jit(solution)/shard_map/psum | solution.py:101
  8.3 22.9 %copy-start.12 = (bf16[1,48,8,8,128]{4,3,2,1,0:T(8,128)(2,1)S(1)}, bf16[1,48,8,8,128]{4,3,2,1,0:T(8,128)(2,1)}, u32[]{:S(2)}) copy-start(bf16[1,48,8,8,128]{4,3,2,1,0:T(8,128)(2,1)} %param.6) | copy-start | bytes 2359300
  8.3 22.9 %collective-permute-start = (bf16[1,48,1,8,128]{4,3,2,1,0:T(8,128)(2,1)S(1)}, bf16[1,48,1,8,128]{4,3,2,1,0:T(8,128)(2,1)S(1)}, u32[]{:S(2)}, u32[]{:S(2)}) collective-permute-start(bf16[1,48,1,8,128]{4,3,2,1,0:T(8,128)(2,1)S(1)} %get-tuple-element.55), channel_id=1, source_target_pairs={{0,32},{32,64},{64,96},{96,128},{128,160},{160,192},{192,224},{1,3... | collective-permute-start | bytes 294920 | tf_op jit(solution)/shard_map/ppermute | solution.py:17
  12.5 18.7 %collective-permute-start.1 = (bf16[1,48,1,8,128]{4,3,2,1,0:T(8,128)(2,1)S(1)}, bf16[1,48,1,8,128]{4,3,2,1,0:T(8,128)(2,1)S(1)}, u32[]{:S(2)}, u32[]{:S(2)}) collective-permute-start(bf16[1,48,1,8,128]{4,3,2,1,0:T(8,128)(2,1)S(1)} %get-tuple-element.56), channel_id=1, source_target_pairs={{32,0},{64,32},{96,64},{128,96},{160,128},{192,160},{224,192},{33,... | collective-permute-start | bytes 294920 | tf_op jit(solution)/shard_map/ppermute | solution.py:19
  15.4 29.1 %collective-permute-start.2 = (bf16[1,48,1,8,128]{4,3,2,1,0:T(8,128)(2,1)}, bf16[1,48,1,8,128]{4,3,2,1,0:T(8,128)(2,1)}, u32[]{:S(2)}, u32[]{:S(2)}) collective-permute-start(bf16[1,48,1,8,128]{4,3,2,1,0:T(8,128)(2,1)} %get-tuple-element.57), channel_id=1, source_target_pairs={{0,32},{32,64},{64,96},{96,128},{128,160},{160,192},{192,224},{1,3... | collective-permute-start | bytes 294920 | tf_op jit(solution)/shard_map/ppermute | solution.py:17
  20.0 24.5 %collective-permute-start.3 = (bf16[1,48,1,8,128]{4,3,2,1,0:T(8,128)(2,1)S(1)}, bf16[1,48,1,8,128]{4,3,2,1,0:T(8,128)(2,1)}, u32[]{:S(2)}, u32[]{:S(2)}) collective-permute-start(bf16[1,48,1,8,128]{4,3,2,1,0:T(8,128)(2,1)S(1)} %get-tuple-element.58), channel_id=1, source_target_pairs={{32,0},{64,32},{96,64},{128,96},{160,128},{192,160},{224,192},{33,... | collective-permute-start | bytes 294920 | tf_op jit(solution)/shard_map/ppermute | solution.py:19
  41.6 2.9 copy-start.6
  42.1 1.5 copy-start.9
  54.0 2.6 copy-start.10
  54.0 2.8 copy-start.13
  54.0 2.8 copy-start.14
  54.5 14.5 %copy-start.8 = (bf16[48,10,8,1,8,17]{0,4,5,2,1,3:T(8,128)(2,1)}, bf16[48,10,8,1,8,17]{0,4,5,2,1,3:T(8,128)(2,1)S(1)}, u32[]{:S(2)}) copy-start(bf16[48,10,8,1,8,17]{0,4,5,2,1,3:T(8,128)(2,1)S(1)} %copy.91) | copy-start | bytes 3133444
  56.9 42.8 %copy-start.16 = (f32[48]{0:T(128)S(1)}, f32[48]{0:T(128)}, u32[]{:S(2)}) copy-start(f32[48]{0:T(128)} %param.10) | copy-start | bytes 580
  56.9 42.8 %copy-start.17 = (f32[48]{0:T(128)S(1)}, f32[48]{0:T(128)}, u32[]{:S(2)}) copy-start(f32[48]{0:T(128)} %param.11) | copy-start | bytes 580
  146.4 7.7 %copy-start.2 = (bf16[48,10,8,1,8,16]{0,2,5,4,1,3:T(8,128)(2,1)S(1)}, bf16[48,10,8,1,8,16]{0,2,5,4,1,3:T(8,128)(2,1)}, u32[]{:S(2)}) copy-start(bf16[48,10,8,1,8,16]{0,2,5,4,1,3:T(8,128)(2,1)} %get-tuple-element.45) | copy-start | bytes 2949124
  148.2 8.2 %copy-start.1 = (bf16[48,10,8,1,8,16]{0,2,5,4,1,3:T(8,128)(2,1)S(1)}, bf16[48,10,8,1,8,16]{0,2,5,4,1,3:T(8,128)(2,1)}, u32[]{:S(2)}) copy-start(bf16[48,10,8,1,8,16]{0,2,5,4,1,3:T(8,128)(2,1)} %get-tuple-element.46) | copy-start | bytes 2949124
  149.5 43.7 %collective-permute-start.6 = (bf16[1,48,1,8,128]{1,0,4,3,2:T(2,128)(2,1)}, bf16[1,48,1,8,128]{1,0,4,3,2:T(2,128)(2,1)}, u32[]{:S(2)}, u32[]{:S(2)}) collective-permute-start(bf16[1,48,1,8,128]{1,0,4,3,2:T(2,128)(2,1)} %bitcast.90), channel_id=1, source_target_pairs={{0,32},{32,64},{64,96},{96,128},{128,160},{160,192},{192,224},{1,3... | collective-permute-start | bytes 294920 | tf_op jit(solution)/shard_map/ppermute | solution.py:17
  152.8 40.3 %collective-permute-start.7 = (bf16[1,48,1,8,128]{1,0,4,3,2:T(2,128)(2,1)}, bf16[1,48,1,8,128]{1,0,4,3,2:T(2,128)(2,1)}, u32[]{:S(2)}, u32[]{:S(2)}) collective-permute-start(bf16[1,48,1,8,128]{1,0,4,3,2:T(2,128)(2,1)} %bitcast.89), channel_id=1, source_target_pairs={{32,0},{64,32},{96,64},{128,96},{160,128},{192,160},{224,192},{33,... | collective-permute-start | bytes 294920 | tf_op jit(solution)/shard_map/ppermute | solution.py:19
  161.5 188.2 %collective-permute-start.4 = (bf16[1,48,1,8,128]{1,3,4,0,2:T(8,128)(2,1)}, bf16[1,48,1,8,128]{1,3,4,0,2:T(8,128)(2,1)}, u32[]{:S(2)}, u32[]{:S(2)}) collective-permute-start(bf16[1,48,1,8,128]{1,3,4,0,2:T(8,128)(2,1)} %slice_bitcast_fusion.3), channel_id=1, source_target_pairs={{0,32},{32,64},{64,96},{96,128},{128,160},{160,192},{192,224},{1,3... | collective-permute-start | bytes 294920 | tf_op jit(solution)/shard_map/ppermute | solution.py:17
  167.0 3.1 copy-start.11
  167.0 182.7 %collective-permute-start.5 = (bf16[1,48,1,8,128]{1,3,4,2,0:T(8,128)(2,1)}, bf16[1,48,1,8,128]{1,3,4,2,0:T(8,128)(2,1)}, u32[]{:S(2)}, u32[]{:S(2)}) collective-permute-start(bf16[1,48,1,8,128]{1,3,4,2,0:T(8,128)(2,1)} %slice_bitcast_fusion.2), channel_id=1, source_target_pairs={{32,0},{64,32},{96,64},{128,96},{160,128},{192,160},{224,192},{33,... | collective-permute-start | bytes 294920 | tf_op jit(solution)/shard_map/ppermute | solution.py:19
  186.8 6.3 copy-start.7
  193.2 75.1 %copy-start.3 = (bf16[8,8,8,17,48]{4,1,3,2,0:T(8,128)(2,1)S(1)}, bf16[8,8,8,17,48]{4,1,3,2,0:T(8,128)(2,1)}, u32[]{:S(2)}) copy-start(bf16[8,8,8,17,48]{4,1,3,2,0:T(8,128)(2,1)} %copy.93) | copy-start | bytes 2506756
  268.2 1.6 copy-start.18
  268.2 1.6 copy-start.19
  268.2 415.9 %all-reduce.8.cloned.1.call-start = ((), (), s32[]{:S(2)}) async-start(), calls=%async_computation | async-start | bytes 2654208 | tf_op jit(solution)/shard_map/psum | solution.py:100
  352.5 52.3 %copy-start.15 = (pred[8,17]{0,1:T(8,128)(4,1)S(1)}, pred[8,17]{0,1:T(8,128)(4,1)}, u32[]{:S(2)}) copy-start(pred[8,17]{0,1:T(8,128)(4,1)} %constant.35) | copy-start | bytes 412
  414.9 1.6 copy-start.4
Sparse Core Ops, SparseCore 0:
  268.3 136.3 all-reduce.9
  407.7 276.3 all-reduce.7
